TPU v7x, 32 devices: a whole 2x2x4 slice. The times are simulated.
32 devices in a mesh: img: 8 (over z, y), head: 4 (over x, core).
Axes of the slice: x: 2, y: 2, z: 4, core: 2. Of those that a mesh axis runs over, the one named last changes fastest.
Arguments:
- tokens: bfloat16 [192, 197, 768], P(('img', 'head')), may hold values from -6 to 6
- slot_ids: int32 [192, 160], P(('img', 'head')), may hold values from 0 to 196, as said below
- counts: int32 [192], P(('img', 'head')), may hold values from 39 to 157
- w_qkv: bfloat16 [768, 2304], P(None, 'head'), may hold values from -0.21875 to 0.21875
- w_out: bfloat16 [768, 768], P('head'), may hold values from -0.875 to 0.875
- w_up: bfloat16 [768, 3072], replicated, may hold values from -0.21875 to 0.21875
- w_down: bfloat16 [3072, 768], replicated, may hold values from -0.109375 to 0.109375
- gain_one: float32 [768], replicated, may hold values from 0.5 to 1.5
- bias_one: float32 [768], replicated, may hold values from -2 to 2
- gain_two: float32 [768], replicated, may hold values from 0.5 to 1.5
- bias_two: float32 [768], replicated, may hold values from -2 to 2
- w_router: float32 [768], replicated, may hold values from -0.21875 to 0.21875
- cotangent: bfloat16 [192, 197, 768], P(('img', 'head')), may hold values from -6 to 6
Outputs:
- result: bfloat16 [192, 197, 768], P(('img', 'head'))
- grad_tokens: float32 [192, 197, 768], P(('img', 'head'))
- grad_qkv: float32 [768, 2304], P(None, 'head')
- grad_out: float32 [768, 768], P('head')
- grad_up: float32 [768, 3072], P(None, 'head')
- grad_down: float32 [3072, 768], P('head')
- grad_gain_one: float32 [768], P('head')
- grad_bias_one: float32 [768], P('head')
- grad_gain_two: float32 [768], P('head')
- grad_bias_two: float32 [768], P('head')
- grad_router: float32 [768], P('head')
Inputs may be any that keep to these rules, and one draw needn't show every extreme that they name: `slot_ids`: within each image the 160 slots hold distinct token numbers; the first counts of them are the routed tokens.
All inputs are finite; a program needn't handle non-finite values.
Results may differ from a plain program's by a relative error of at most 0.012.
The roundings to bfloat16 on the way count: a program that leaves them out, or rounds other values in their place, can miss the bound.
Values may be sent and summed in bfloat16 or wider, within the bound.
A program may use at most 256 MiB of HBM per device.

v0:
```python
import functools

import jax
import jax.numpy as jnp
from jax import lax
from jax.experimental import pallas as pl
from jax.experimental.pallas import tpu as pltpu
from jax.sharding import PartitionSpec as P

HEAD_DIM = 64
EPS = 1e-06
BF = jnp.bfloat16
F32 = jnp.float32


def nn(a, b):
    return lax.dot_general(a, b, (((1,), (0,)), ((), ())), preferred_element_type=F32)


def nt(a, b):
    return lax.dot_general(a, b, (((1,), (1,)), ((), ())), preferred_element_type=F32)


def tn(a, b):
    return lax.dot_general(a, b, (((0,), (0,)), ((), ())), preferred_element_type=F32)


def standardise(values):
    average = jnp.mean(values, axis=-1, keepdims=True)
    centred = values - average
    variance = jnp.mean(centred * centred, axis=-1, keepdims=True)
    scale = lax.rsqrt(variance + EPS)
    return centred * scale, scale


def norm_pull(grad, unit, scale, gain):
    inner = grad * gain
    first = jnp.mean(inner, axis=-1, keepdims=True)
    second = jnp.mean(inner * unit, axis=-1, keepdims=True)
    return scale * (inner - first - unit * second)


def split_low(values):
    upper = values.astype(BF)
    return upper, (values - upper.astype(F32)).astype(BF)


def slot_table(slots, length):
    capacity = slots.shape[1]
    return (lax.broadcasted_iota(jnp.int32, (length, capacity), 0) == slots).astype(BF)


def row_gate(picked, w_router, count):
    gate = jax.nn.sigmoid(jnp.sum(picked * w_router, axis=-1, keepdims=True))
    valid = (lax.broadcasted_iota(jnp.int32, gate.shape, 0) < count).astype(F32)
    return gate, valid


def lane_low(shape):
    return lax.broadcasted_iota(jnp.int32, shape, 1) < HEAD_DIM


def head_scores(key_tile, query_tile, low, count):
    scores = nt(key_tile, query_tile)
    seen = lax.broadcasted_iota(jnp.int32, scores.shape, 0) < count
    return jnp.where(seen, scores, -1e30)


def swap_halves(tile):
    return pltpu.roll(tile.astype(F32), HEAD_DIM, 1).astype(BF)


def pair_lanes(pair, t):
    return pl.ds(pl.multiple_of((3 * pair + t) * 2 * HEAD_DIM, 128), 2 * HEAD_DIM)


def pair_tiles(proj, rows, pair):
    tiles = [proj[rows, pair_lanes(pair, t)] for t in range(3)]
    low = lane_low(tiles[0].shape)
    zero = jnp.zeros_like(tiles[0])
    swapped = [swap_halves(tile) for tile in tiles]
    scale = HEAD_DIM ** (-0.5)
    query_a = jnp.where(low, tiles[0], zero) * jnp.asarray(scale, BF)
    query_b = jnp.where(low, swapped[1], zero) * jnp.asarray(scale, BF)
    return tiles, swapped, low, zero, ((swapped[0], query_a), (tiles[2], query_b))

MESH_ID = pl.DeviceIdType.MESH
AG_ROWS = 96


def copy_in(source, target, sem):
    copy = pltpu.make_async_copy(source, target, sem)
    copy.start()
    return copy


def aligned(start, size, unit=16):
    return pl.ds(pl.multiple_of(start, unit), size)


class Place:
    def __init__(self, outer):
        self.head = lax.axis_index("head")
        self.img = lax.axis_index("img")
        self.outer = outer
        self.x, self.c = self.head // 2, self.head % 2
        self.z, self.y = self.img // 2, self.img % 2
        self.own = self.head
        self.across = 2 * (1 - self.x) + self.c
        self.core_at = (self.img, 2 * self.x + 1 - self.c)
        self.x_at = (self.img, self.across)
        self.y_at = (2 * self.z + 1 - self.y, self.head)
        self.z_at = []
        self.z_of = []
        for k in range(1, outer):
            other = lax.rem(self.z + k, outer)
            self.z_of.append(other)
            self.z_at.append((2 * other + self.y, self.head))


def remote(source, target, sems, index, device):
    return pltpu.make_async_remote_copy(
        src_ref=source,
        dst_ref=target,
        send_sem=sems[0].at[index],
        recv_sem=sems[1].at[index],
        device_id=device,
        device_id_type=MESH_ID,
    )


def send(source, target, sems, index, device):
    copy = remote(source, target, sems, index, device)
    copy.start()
    return copy


class Gather:
    def __init__(self, place, whole, w_qkv_t, w_out, sems, local_sems):
        self.p, self.whole, self.sems = place, whole, sems
        self.w = (w_qkv_t, w_out)
        self.sizes = (w_qkv_t.shape[0], w_out.shape[0])
        self.columns = 4 * self.sizes[0]
        self.local_sems = local_sems
        self.split = (self.sizes[0] // 2) // AG_ROWS
        self.steps = self.split + 1

    def part(self, shard, kind, first=0, size=None):
        base = shard * self.sizes[kind] + (self.columns if kind else 0) + first
        return self.whole.at[aligned(base, size or self.sizes[kind])]

    def first_row(self, side, t):
        return side * AG_ROWS if t == self.split else (self.split * side + t) * AG_ROWS

    def piece(self, shard, side, t):
        return self.part(shard, int(t == self.split), self.first_row(side, t), AG_ROWS)

    def source(self, side, t):
        return self.w[int(t == self.split)].at[aligned(self.first_row(side, t), AG_ROWS)]

    def local(self, k):
        return pltpu.make_async_copy(self.w[k], self.part(self.p.own, k), self.local_sems.at[k])

    def core(self, k):
        return remote(self.w[k], self.part(self.p.own, k), self.sems, k, self.p.core_at)

    def over_x(self, t):
        p = self.p
        return remote(self.source(p.y, t), self.piece(p.own, p.y, t), self.sems, 2 + t, p.x_at)

    def over_y(self, t):
        p = self.p
        block = self.piece(p.across, p.y, t)
        return remote(block, block, self.sems, 2 + self.steps + t, p.y_at)

    def passed(self, t):
        p, n = self.p, self.steps
        side = p.y if t < n else 1 - p.y
        block = self.piece(p.across, side, t % n)
        return remote(block, block, self.sems, 2 + 2 * n + t, p.core_at)

    def begin(self):
        for k in range(2):
            self.local(k).start()
            self.core(k).start()
        for t in range(self.steps):
            self.over_x(t).start()

    def own_half(self):
        for k in range(2):
            self.local(k).wait()
            self.core(k).wait_recv()

    def forward_x(self, t):
        self.over_x(t).wait_recv()
        self.over_y(t).start()
        self.passed(t).start()

    def forward_y(self, t):
        self.over_y(t).wait_recv()
        self.passed(self.steps + t).start()

    def other_half(self, steps):
        for t in steps:
            self.passed(t).wait_recv()
            self.passed(self.steps + t).wait_recv()

    def close(self):
        for k in range(2):
            self.core(k).wait_send()
        for t in range(self.steps):
            self.over_x(t).wait_send()
            self.over_y(t).wait_send()
        for t in range(2 * self.steps):
            self.passed(t).wait_send()


def add_into(block, *others):
    rows = 64 if block.shape[0] % 64 == 0 else 16

    @pl.loop(0, block.shape[0] // rows)
    def _(n):
        part = aligned(n * rows, rows)
        total = block[part, :].astype(F32)
        for other in others:
            total += other[part, :].astype(F32)
        block[part, :] = total.astype(BF)


class Reduce:
    def __init__(self, place, jobs, out, buffers, sems, local_sem):
        self.p, self.out = place, out
        self.blocks = [job[0] for job in jobs]
        self.rows = [job[1] for job in jobs]
        self.target = [job[2] for job in jobs]
        self.base = [sum(self.rows[:j]) for j in range(len(jobs))]
        self.from_core, self.from_x, self.from_y, self.from_z = buffers
        self.core_sems, self.x_sems, self.y_sems, self.z_sems, self.az_sems, self.ay_sems = sems
        self.local_sem = local_sem
        self.jobs = len(jobs)
        self.sent = []
        self.kept = []
        self.core, self.over_x, self.over_y = {}, {}, {}
        self.over_z, self.all_z, self.all_y = {}, {}, {}
        self.half = out.shape[1] // 2
        self.mine = aligned(place.y * self.half, self.half, 128)
        self.theirs = aligned((1 - place.y) * self.half, self.half, 128)

    def span(self, j):
        return slice(self.base[j], self.base[j] + self.rows[j])

    def ready(self, j):
        p = self.p
        shards = [(1 - p.x), p.x]
        self.core[j] = [
            send(
                self.blocks[j](2 * xx + 1 - p.c), self.from_core.at[xx, self.span(j)],
                self.core_sems, (j, n), p.core_at,
            )
            for n, xx in enumerate(shards)
        ]
        self.sent += self.core[j]

    def to_x(self, j):
        p = self.p
        self.core[j][0].wait_recv()
        block = self.blocks[j](p.across)
        add_into(block, self.from_core.at[1 - p.x, self.span(j)])
        self.over_x[j] = send(block, self.from_x.at[self.span(j)], self.x_sems, j, p.x_at)
        self.sent.append(self.over_x[j])

    def to_y(self, j):
        p = self.p
        self.core[j][1].wait_recv()
        self.over_x[j].wait_recv()
        block = self.blocks[j](p.own)
        add_into(block, self.from_core.at[p.x, self.span(j)], self.from_x.at[self.span(j)])
        self.over_y[j] = send(
            block.at[:, self.theirs], self.from_y.at[self.span(j)], self.y_sems, j, p.y_at
        )
        self.sent.append(self.over_y[j])

    def quarters(self, j):
        size = self.rows[j] // self.p.outer
        base = self.base[j] // self.p.outer
        return size, slice(base, base + size)

    def to_z(self, j):
        p = self.p
        self.over_y[j].wait_recv()
        block = self.blocks[j](p.own).at[:, self.mine]
        add_into(block, self.from_y.at[self.span(j)])
        size, span = self.quarters(j)
        self.over_z[j] = [
            send(
                block.at[aligned(size * p.z_of[k], size)], self.from_z.at[k, span],
                self.z_sems, (j, k), p.z_at[k],
            )
            for k in range(p.outer - 1)
        ]
        self.sent += self.over_z[j]

    def place_of(self, j, z, lanes):
        size, _ = self.quarters(j)
        return self.out.at[aligned(self.target[j] + size * z, size), lanes]

    def spread(self, j):
        p = self.p
        for copy in self.over_z[j]:
            copy.wait_recv()
        size, span = self.quarters(j)
        piece = self.blocks[j](p.own).at[aligned(size * p.z, size), self.mine]
        add_into(piece, *[self.from_z.at[k, span] for k in range(p.outer - 1)])
        target = self.place_of(j, p.z, self.mine)
        self.kept.append(copy_in(piece, target, self.local_sem.at[j]))
        self.all_z[j] = [
            send(piece, target, self.az_sems, (j, k), p.z_at[k]) for k in range(p.outer - 1)
        ]
        self.all_y[j] = [send(piece, target, self.ay_sems, (j, 0), p.y_at)]
        self.sent += self.all_z[j] + self.all_y[j]

    def across_y(self, j):
        p = self.p
        for k in range(p.outer - 1):
            self.all_z[j][k].wait_recv()
            z = lax.rem(p.z + p.outer - 1 - k, p.outer)
            block = self.place_of(j, z, self.mine)
            copy = send(block, block, self.ay_sems, (j, k + 1), p.y_at)
            self.all_y[j].append(copy)
            self.sent.append(copy)

    def finish(self, j):
        for copy in self.all_y[j]:
            copy.wait_recv()

    def feed(self, last):
        for j in range(min(last + 1, self.jobs)):
            if j in self.core and j not in self.over_x:
                self.to_x(j)

    def tick(self, t):
        for lag, step in enumerate((self.to_y, self.to_z, self.spread, self.across_y, self.finish)):
            if 0 <= t - lag < self.jobs:
                step(t - lag)

    def close(self):
        for copy in self.sent:
            copy.wait_send()
        for copy in self.kept:
            copy.wait()


def sum_vectors(place, vec, inbox, sems, sent):
    p = place
    partners = [p.core_at, p.x_at, p.y_at]
    bit = 1
    while bit < p.outer:
        low = lax.rem(p.z // bit, 2)
        partners.append((2 * (p.z + bit - 2 * bit * low) + p.y, p.head))
        bit *= 2
    count = len(partners)
    copies = []

    def stage(n):
        if n:
            copies[n - 1].wait_recv()
            vec[n] = vec[n - 1] + inbox[n - 1]
        if n < count:
            copies.append(send(vec.at[n], inbox.at[n], sems, n, partners[n]))
            sent.append(copies[n])

    return [functools.partial(stage, n) for n in range(count + 1)]


def fused_kernel(owned, length, capacity, parts, outer, names, *refs):
    r = dict(zip(names, refs))
    remote = outer > 0
    slots, counts = r["slots"], r["counts"]
    gain_one, bias_one, gain_two, bias_two, w_router = (
        r[k][...][None, :] for k in ("gain_one", "bias_one", "gain_two", "bias_two", "w_router")
    )
    tokens, cotangent = r["tokens"], r["cotangent"]
    wu, wd, ra, rs, down = r["wu"], r["wd"], r["ra"], r["rs"], r["down"]
    normed_two, grad_mlp, mixed, attn, wide = (
        r[k] for k in ("normed_two", "grad_mlp", "mixed", "attn", "wide")
    )
    picked, picked_grad, totals, logits = (r[k] for k in ("picked", "picked_grad", "totals", "logits"))
    tok, cot, res, gtok = (r[k] for k in ("tok", "cot", "res", "gtok"))
    sems, tok_sems, cot_sems, res_sems, gtok_sems = (
        r[k] for k in ("sems", "tok_sems", "cot_sems", "res_sems", "gtok_sems")
    )
    result_o, grad_tokens_o, saved_o, vec_o = (
        r[k] for k in ("result_o", "grad_tokens_o", "saved_o", "vec_o")
    )
    vec = r["vec"]
    features, hidden = wu.shape
    columns = wd.shape[0] - features
    pairs = columns // (6 * HEAD_DIM)
    proj = ra.at[:, 0:columns]
    normed_one = ra.at[:, columns : columns + features]
    width = features // 3
    part = hidden // parts
    rows_all = owned * capacity
    piece = features // 3

    def rows_of(i):
        return aligned(i * capacity, capacity)

    def slot_row(i):
        return slots[pl.ds(i, 1), :]

    def token_copy(i, slot):
        return pltpu.make_async_copy(tokens.at[i], tok.at[slot], tok_sems.at[slot])

    def cot_copy(i, slot):
        return pltpu.make_async_copy(cotangent.at[i], cot.at[slot], cot_sems.at[slot])

    def result_copy(i, slot):
        return pltpu.make_async_copy(res.at[slot], result_o.at[i], res_sems.at[slot])

    def gtok_copy(i, slot):
        return pltpu.make_async_copy(gtok.at[slot], grad_tokens_o.at[i], gtok_sems.at[slot])

    token_copy(0, 0).start()
    cot_copy(0, 0).start()
    reduce = None
    if remote:
        place = Place(outer)
        barrier = pltpu.get_barrier_semaphore()
        partners = [place.core_at, place.x_at, place.y_at, *place.z_at]
        for partner in partners:
            pl.semaphore_signal(barrier, inc=1, device_id=partner, device_id_type=MESH_ID)
        pl.semaphore_wait(barrier, len(partners))
        gather = Gather(
            place, down, r["w_qkv_t"], r["w_out"], (r["ag_send"], r["ag_recv"]), r["local_sems"]
        )
        gather.begin()
        w_all = r["w_saved_o"]
        half_order = (place.x, 1 - place.x)

        def rows_block(ref, base, step, rows):
            return lambda s: ref.at[aligned(s * step + base, rows)]

        def lanes_block(ref, base, rows):
            return lambda s: ref.at[base : base + rows, aligned(s * part, part, 128)]

        def head_block(ref, q, rows):
            return lambda s: ref.at[aligned(s * share + lax.rem(q + s % 2, 3) * rows, rows)]

        share = columns // parts
        out_rows = features // parts
        jobs = [
            (rows_block(down, piece * k, part, piece), piece, piece * k) for k in range(part // piece)
        ]
        jobs += [
            (lanes_block(wu, features // 2 * k, features // 2), features // 2, part + features // 2 * k)
            for k in range(2)
        ]
        after = part + features
        jobs += [(rows_block(wd, columns, out_rows, out_rows), out_rows, after)]
        after += out_rows
        jobs += [
            (head_block(wd, q, share // 3), share // 3, after + lax.rem(q + place.c, 3) * (share // 3))
            for q in range(3)
        ]
        reduce = Reduce(
            place, jobs, r["grads_o"], [r[k] for k in ("from_core", "from_x", "from_y", "from_z")],
            [(r[k + "_send"], r[k + "_recv"]) for k in ("core", "x", "y", "z", "az", "ay")],
            r["kept_sems"],
        )
        job_down, job_up = part // piece, 2
    else:
        job_down, job_up = part // piece, 2
        w_all = r["w_all"]
        load_w = copy_in(w_all, down, sems.at[0])
        half_order = (0, 1)
    load_up = copy_in(r["w_up"], wu, sems.at[1])
    load_down = copy_in(r["w_down"], wd, sems.at[2])
    ticks = [0]

    def tick():
        if remote:
            reduce.tick(ticks[0])
            ticks[0] += 1

    @pl.loop(0, owned)
    def _(i):
        slot = lax.rem(i, 2)

        @pl.when(i + 1 < owned)
        def _():
            token_copy(i + 1, 1 - slot).start()
            cot_copy(i + 1, 1 - slot).start()

        rows = rows_of(i)
        table = slot_table(slot_row(i), length)
        token_copy(i, slot).wait()
        rows_f = tn(table, tok[slot])
        picked[rows, :] = rows_f.astype(BF)
        unit, _ = standardise(rows_f)
        normed_one[rows, :] = (unit * gain_one + bias_one).astype(BF)
        gate, valid = row_gate(rows_f, w_router, counts[i])
        cot_copy(i, slot).wait()
        grads = tn(table, cot[slot])
        picked_grad[rows, :] = grads.astype(BF)
        grad_mlp[rows, :] = (gate * valid * grads).astype(BF)

    def project(half):
        base = pl.multiple_of(half * (columns // 2), 128)
        size = rows_all // 3

        @pl.loop(0, 3)
        def _(n):
            rows = aligned(n * size, size)
            proj[rows, pl.ds(base, columns // 2)] = nt(
                normed_one[rows, :], down[pl.ds(base, columns // 2), :]
            ).astype(BF)

    def attend(half, i):
        rows = rows_of(i)
        for p in range(pairs // 2):
            pair = half * (pairs // 2) + p
            tiles, swapped, low, zero, heads = pair_tiles(proj, rows, pair)
            outs = []
            for h, (key_tile, query_tile) in enumerate(heads):
                scores = head_scores(key_tile, query_tile, low, counts[i])
                highest = jnp.max(scores, axis=0, keepdims=True)
                terms = jnp.exp(scores - highest)
                total = jnp.sum(terms, axis=0, keepdims=True)
                probs = (terms * (1.0 / total)).astype(BF)
                totals[i, pl.ds(2 * pair + h, 1), :] = highest + jnp.log(total)
                outs.append(tn(probs, tiles[1 + h]))
            mixed[rows, aligned(2 * HEAD_DIM * pair, 2 * HEAD_DIM, 128)] = jnp.where(
                low, outs[0], outs[1]
            ).astype(BF)

    if remote:
        gather.forward_x(0)
        gather.own_half()
    else:
        load_w.wait()

    @pl.loop(0, 2)
    def _(turn):
        if remote:
            half = place.x + turn - 2 * place.x * turn

            @pl.when(turn == 1)
            def _():
                gather.forward_y(2)
                gather.other_half(range(gather.split))
        else:
            half = turn
        project(half)

        @pl.loop(0, owned)
        def _(i):
            if remote:
                for at, steps in ((0, ((0, 1),)), (2, ((0, 2), (1, 0))), (4, ((1, 1),))):

                    @pl.when((turn == 0) & (i == at))
                    def _(steps=steps):
                        for kind, t in steps:
                            (gather.forward_y if kind else gather.forward_x)(t)

                @pl.when((turn == 1) & (i == 0))
                def _():
                    gather.forward_x(3)

                @pl.when((turn == 1) & (i == 3))
                def _():
                    gather.forward_y(3)

            attend(half, i)

    if remote:
        gather.other_half((gather.split,))
        keep_w = copy_in(down, w_all, sems.at[0])
    save = copy_in(ra, saved_o, sems.at[3])

    @pl.loop(0, 3)
    def _(n):
        cols = aligned(n * width, width, 128)
        attn[:, cols] = nn(mixed[...], down[columns : columns + features, cols])

    @pl.loop(0, owned)
    def _(i):
        rows = rows_of(i)
        unit, _ = standardise(picked[rows, :].astype(F32) + attn[rows, :])
        normed_two[rows, :] = (unit * gain_two + bias_two).astype(BF)

    save.wait()
    load_up.wait()
    step = hidden // 6
    for k in range(part // piece):

        @pl.loop(0, parts)
        def _(h):
            cols = aligned(h * part + k * piece, piece, 128)
            pre = nn(normed_two[...], wu[:, cols])
            below = 0.5 + 0.5 * lax.erf(pre * (0.5**0.5))
            ra[:, cols] = (pre * below).astype(BF)
            rs[:, cols] = (below + pre * (jnp.exp(-0.5 * pre * pre) * 0.3989422804014327)).astype(BF)

        if remote and k == 0:
            gather.close()
            keep_w.wait()
        if remote and k:
            reduce.feed(k - 1)

        @pl.loop(0, parts)
        def _(h):
            cols = aligned(h * part + k * piece, piece, 128)
            down[cols, :] = tn(ra[:, cols], grad_mlp[...]).astype(BF)

        if remote:
            reduce.ready(k)

    if not remote:
        put_down = copy_in(down, r["down_o"], sems.at[4])
    load_down.wait()

    @pl.loop(0, 6)
    def _(n):
        cols = aligned(n * step, step, 128)
        rs[:, cols] = (nt(grad_mlp[...], wd[cols, :]) * rs[:, cols].astype(F32)).astype(BF)

    if remote:
        reduce.feed(job_down - 1)

    @pl.loop(0, 3)
    def _(n):
        cols = aligned(n * width, width, 128)
        wide[:, cols] = nt(rs[...], wu[cols, :])

    tick()
    step_up = features // job_up
    for k in range(job_up):

        @pl.loop(0, parts)
        def _(h):
            cols = aligned(h * part, part, 128)
            rows = slice(k * step_up, (k + 1) * step_up)
            wu[rows, cols] = tn(normed_two[:, rows], rs[:, cols]).astype(BF)

        if remote:
            if k:
                reduce.feed(job_down + k - 1)
            reduce.ready(job_down + k)

    tick()
    if not remote:
        put_up = copy_in(wu, r["up_o"], sems.at[5])

    blocks = [copy_in(w_all.at[columns : columns + features], rs.at[0:features, 0:features], sems.at[6])]
    for n in range(3):
        blocks.append(
            copy_in(
                w_all.at[n * features : (n + 1) * features],
                rs.at[0:features, (n + 1) * features : (n + 2) * features],
                sems.at[7 + n],
            )
        )

    vec[0] = jnp.zeros_like(vec[0])

    @pl.loop(0, owned)
    def _(i):
        rows = rows_of(i)
        rows_f = picked[rows, :].astype(F32)
        unit, scale = standardise(rows_f + attn[rows, :])
        grad = wide[rows, :]
        vec[0, 2:3, :] += jnp.sum(grad * unit, axis=0, keepdims=True)
        vec[0, 3:4, :] += jnp.sum(grad, axis=0, keepdims=True)
        wide[rows, :] = norm_pull(grad, unit, scale, gain_two)

    @pl.loop(0, 3)
    def _(n):
        cols = aligned(n * width, width, 128)
        attn[:, cols] += nn(ra[...], wd[:, cols])

    reload = copy_in(saved_o, ra, sems.at[3])
    if remote:
        reduce.feed(job_down + job_up - 1)
    tick()

    @pl.loop(0, owned)
    def _(i):
        rows = rows_of(i)
        rows_f = picked[rows, :].astype(F32)
        gate, valid = row_gate(rows_f, w_router, counts[i])
        grads = picked_grad[rows, :].astype(F32)
        logit = valid * gate * (1.0 - gate) * jnp.sum(grads * attn[rows, :], axis=-1, keepdims=True)
        logits[rows, :] = jnp.broadcast_to(logit, (capacity, 128))
        vec[0, 4:5, :] += jnp.sum(logit * rows_f, axis=0, keepdims=True)
        grad_mlp[rows, :] = (gate * valid * grads + wide[rows, :]).astype(BF)

    @pl.loop(0, 3)
    def _(n):
        cols = aligned(n * width, width, 128)
        wd[columns : columns + features, cols] = tn(mixed[...], grad_mlp[:, cols]).astype(BF)

    if remote:
        reduce.ready(job_down + job_up)
    blocks[0].wait()
    @pl.loop(0, 3)
    def _(n):
        cols = aligned(n * width, width, 128)
        normed_two[:, cols] = nt(grad_mlp[...], rs[cols, 0:features]).astype(BF)

    tick()
    reload.wait()

    def attend_back(chosen, first, last):
        @pl.loop(first, last)
        def _(i):
            rows = rows_of(i)
            for pair in chosen:
                tiles, swapped, low, zero, heads = pair_tiles(proj, rows, pair)
                lanes = slice(2 * HEAD_DIM * pair, 2 * HEAD_DIM * (pair + 1))
                grads = normed_two[rows, lanes]
                halves = (jnp.where(low, grads, zero), jnp.where(low, zero, grads))
                found = []
                for h, (key_tile, query_tile) in enumerate(heads):
                    scores = head_scores(key_tile, query_tile, low, counts[i])
                    probs = jnp.exp(scores - totals[i, 2 * pair + h : 2 * pair + h + 1, :])
                    grad_probs = nt(tiles[1 + h], halves[h])
                    shift = jnp.sum(probs * grad_probs, axis=0, keepdims=True)
                    grad_scores = (probs * (grad_probs - shift)).astype(BF)
                    grad_value = nn(probs.astype(BF), grads)
                    scale = HEAD_DIM ** (-0.5)
                    grad_query = tn(grad_scores, swapped[2 * h]) * scale
                    grad_key = nn(grad_scores, swapped[h]) * scale
                    found.append((grad_query, grad_key, grad_value))
                (query_a, key_a, value_a), (query_b, key_b, value_b) = found
                proj[rows, pair_lanes(pair, 0)] = jnp.where(low, query_a, key_a).astype(BF)
                proj[rows, pair_lanes(pair, 1)] = jnp.where(low, value_a, query_b).astype(BF)
                proj[rows, pair_lanes(pair, 2)] = jnp.where(low, key_b, value_b).astype(BF)

    early = [p for p in range(pairs) if p % 3 != 1]
    late = [p for p in range(pairs) if p % 3 == 1]

    def grad_qkv(count, pair_at):
        @pl.loop(0, count)
        def _(n):
            cols = aligned(pair_at(n) * 6 * HEAD_DIM, 6 * HEAD_DIM, 128)
            wd[cols, :] = tn(proj[:, cols], normed_one[...]).astype(BF)

    if remote:
        reduce.feed(job_down + job_up)
    attend_back(early, 0, owned // 2)
    tick()
    attend_back(early, owned // 2, owned)
    grad_qkv(len(early), lambda n: n + (n + 1) // 2)
    first_qkv = job_down + job_up + 1 if remote else 0
    if remote:
        reduce.ready(first_qkv)
        reduce.ready(first_qkv + 1)
    tick()
    attend_back(late, 0, owned // 2)
    if remote:
        reduce.feed(first_qkv + 1)
    attend_back(late, owned // 2, owned)
    grad_qkv(len(late), lambda n: 3 * n + 1)
    if remote:
        reduce.ready(first_qkv + 2)
    else:
        put_qkv = copy_in(wd, r["qkv_out_o"], sems.at[0])

    for n in range(3):
        blocks[1 + n].wait()
    token_copy(0, 0).start()

    def put_results(first, last):
        @pl.loop(first, last)
        def _(i):
            slot = lax.rem(i, 2)

            @pl.when(i + 1 < owned)
            def _():
                token_copy(i + 1, 1 - slot).start()

            rows = rows_of(i)
            gate, valid = row_gate(picked[rows, :].astype(F32), w_router, counts[i])
            table = slot_table(slot_row(i), length)
            upper, lower = split_low(gate * valid * attn[rows, :])
            token_copy(i, slot).wait()

            @pl.when(i >= 2)
            def _():
                result_copy(i - 2, slot).wait()

            res[slot] = (tok[slot].astype(F32) + (nn(table, upper) + nn(table, lower))).astype(BF)
            result_copy(i, slot).start()

    put_results(0, owned // 2)
    if remote:
        reduce.feed(first_qkv + 2)
    tick()
    put_results(owned // 2, owned)

    @pl.loop(0, 3)
    def _(n):
        cols = aligned(n * width, width, 128)
        total = nn(proj[:, 0:features], rs[0:features, aligned(features + n * width, width, 128)])
        for k in range(1, 3):
            total += nn(
                proj[:, k * features : (k + 1) * features],
                rs[0:features, aligned((k + 1) * features + n * width, width, 128)],
            )
        attn[:, cols] = total

    tick()
    cot_copy(0, 0).start()

    @pl.loop(0, owned)
    def _(i):
        slot = lax.rem(i, 2)

        @pl.when(i + 1 < owned)
        def _():
            cot_copy(i + 1, 1 - slot).start()

        rows = rows_of(i)
        rows_f = picked[rows, :].astype(F32)
        unit, scale = standardise(rows_f)
        grad = attn[rows, :]
        vec[0, 0:1, :] += jnp.sum(grad * unit, axis=0, keepdims=True)
        vec[0, 1:2, :] += jnp.sum(grad, axis=0, keepdims=True)
        back = norm_pull(grad, unit, scale, gain_one)
        total = back + wide[rows, :] + logits[rows, 0:1] * w_router
        table = slot_table(slot_row(i), length)
        upper, lower = split_low(total)
        cot_copy(i, slot).wait()

        @pl.when(i >= 2)
        def _():
            gtok_copy(i - 2, slot).wait()

        gtok[slot] = cot[slot].astype(F32) + (nn(table, upper) + nn(table, lower))
        gtok_copy(i, slot).start()

    if remote:
        stages = sum_vectors(place, vec, r["vec_in"], (r["vec_send"], r["vec_recv"]), reduce.sent)
        while ticks[0] < reduce.jobs + 4:
            if stages:
                stages.pop(0)()
            tick()
        while stages:
            stages.pop(0)()
        vec_o[...] = vec[vec.shape[0] - 1]
    else:
        vec_o[...] = vec[0]

    for i in range(max(owned - 2, 0), owned):
        result_copy(i, i % 2).wait()
        gtok_copy(i, i % 2).wait()
    if remote:
        reduce.close()
    else:
        put_down.wait()
        put_up.wait()
        put_qkv.wait()


def finish_kernel(sizes, *refs):
    grads, result, grad_tokens = refs[:3]
    outs, result_o, grad_tokens_o = refs[3:7], refs[7], refs[8]
    narrow, wide, kept_rows, kept_grads, in_sems, out_sems, row_sems = refs[9:]
    rows_in = [copy_in(result, kept_rows, row_sems.at[0]), copy_in(grad_tokens, kept_grads, row_sems.at[1])]
    chunk = 192
    places = [(out, r) for out, size in zip(outs, sizes) for r in range(0, size, chunk)]
    loads, copies = [], []
    for n in range(len(places)):
        rows = slice(n * chunk, (n + 1) * chunk)
        loads.append(copy_in(grads.at[rows], narrow.at[rows], in_sems.at[n]))
    for n, (out, r) in enumerate(places):
        rows = slice(n * chunk, (n + 1) * chunk)
        loads[n].wait()
        wide[rows, :] = narrow[rows, :].astype(F32)
        copies.append(copy_in(wide.at[rows], out.at[r : r + chunk], out_sems.at[n]))
        if n == 0:
            rows_in[0].wait()
            copies.append(copy_in(kept_rows, result_o, row_sems.at[2]))
            rows_in[1].wait()
            copies.append(copy_in(kept_grads, grad_tokens_o, row_sems.at[3]))
    for copy in copies:
        copy.wait()


def finish(grads, sizes, result, grad_tokens):
    total, features = grads.shape
    outside = pl.BlockSpec(memory_space=pltpu.HBM)
    S = jax.ShapeDtypeStruct
    D = pltpu.SemaphoreType.DMA
    shapes = [S((size, features), F32) for size in sizes]
    shapes += [S(result.shape, result.dtype), S(grad_tokens.shape, grad_tokens.dtype)]
    return pl.pallas_call(
        functools.partial(finish_kernel, sizes),
        out_shape=shapes,
        in_specs=[outside] * 3,
        out_specs=[outside] * len(shapes),
        scratch_shapes=[
            pltpu.VMEM((total, features), BF), pltpu.VMEM((total, features), F32),
            pltpu.VMEM(result.shape, BF), pltpu.VMEM(grad_tokens.shape, F32),
            D((total // 192,)), D((total // 192,)), D((4,)),
        ],
        compiler_params=pltpu.CompilerParams(vmem_limit_bytes=60 << 20),
    )(grads, result, grad_tokens)


def fused(
    parts, outer, tokens, slot_ids, counts, weights, w_up, w_down,
    gain_one, bias_one, gain_two, bias_two, w_router, cotangent,
):
    owned, length, features = tokens.shape
    capacity = slot_ids.shape[1]
    rows = owned * capacity
    hidden = w_up.shape[1]
    remote = outer > 0
    columns = weights[0].shape[0] * parts if remote else weights[0].shape[0] - features
    heads = columns // (3 * HEAD_DIM)
    S = jax.ShapeDtypeStruct
    inside = pl.BlockSpec(memory_space=pltpu.VMEM)
    outside = pl.BlockSpec(memory_space=pltpu.HBM)
    scalars = pl.BlockSpec(memory_space=pltpu.SMEM)
    V = pltpu.VMEM
    D = pltpu.SemaphoreType.DMA
    ins = {
        "slots": (slot_ids, inside), "counts": (counts, scalars),
        "gain_one": (gain_one, inside), "bias_one": (bias_one, inside), "gain_two": (gain_two, inside),
        "bias_two": (bias_two, inside), "w_router": (w_router, inside),
        "tokens": (tokens, outside), "cotangent": (cotangent, outside),
        "w_up": (w_up, outside), "w_down": (w_down, outside),
    }
    outs = {
        "result_o": (S((owned, length, features), BF), outside),
        "grad_tokens_o": (S((owned, length, features), F32), outside),
        "vec_o": (S((8, features), F32), inside),
        "saved_o": (S((rows, columns + features), BF), outside),
    }
    steps = 3
    if remote:
        steps = 3 + outer.bit_length() - 1
    scratch = {
        "wu": V((features, hidden), BF), "wd": V((hidden, features), BF), "ra": V((rows, hidden), BF),
        "rs": V((rows, hidden), BF), "down": V((hidden, features), BF),
        "normed_two": V((rows, features), BF), "grad_mlp": V((rows, features), BF),
        "mixed": V((rows, features), BF), "attn": V((rows, features), F32), "wide": V((rows, features), F32),
        "picked": V((rows, features), BF), "picked_grad": V((rows, features), BF),
        "totals": V((owned, heads, capacity), F32), "logits": V((rows, 128), F32),
        "tok": V((2, length, features), BF), "cot": V((2, length, features), BF),
        "res": V((2, length, features), BF), "gtok": V((2, length, features), F32),
        "vec": V((steps + 1, 8, features), F32),
        "sems": D((10,)), "tok_sems": D((2,)), "cot_sems": D((2,)), "res_sems": D((2,)), "gtok_sems": D((2,)),
    }
    if remote:
        ins["w_qkv_t"] = (weights[0], outside)
        ins["w_out"] = (weights[1], outside)
        outs["w_saved_o"] = (S((columns + features, features), BF), outside)
        total = (columns + features + 2 * hidden) // parts
        jobs = 9
        outs["grads_o"] = (S((total, features), BF), outside)
        half = features // 2
        scratch.update({
            "from_core": V((2, total, features), BF), "from_x": V((total, features), BF),
            "from_y": V((total, half), BF), "from_z": V((outer - 1, total // outer, half), BF),
            "vec_in": V((steps, 8, features), F32),
            "local_sems": D((2,)), "kept_sems": D((jobs,)),
        })
        for name, shape in (
            ("ag", (18,)), ("core", (jobs, 2)), ("x", (jobs,)), ("y", (jobs,)), ("z", (jobs, outer - 1)),
            ("az", (jobs, outer - 1)), ("ay", (jobs, outer)), ("vec", (steps,)),
        ):
            scratch[name + "_send"] = D(shape)
            scratch[name + "_recv"] = D(shape)
    else:
        ins["w_all"] = (weights[0], outside)
        outs["down_o"] = (S((hidden, features), BF), outside)
        outs["up_o"] = (S((features, hidden), BF), outside)
        outs["qkv_out_o"] = (S((columns + features, features), BF), outside)
    names = list(ins) + list(outs) + list(scratch)
    found = pl.pallas_call(
        functools.partial(fused_kernel, owned, length, capacity, parts, outer, names),
        out_shape=[v[0] for v in outs.values()],
        in_specs=[v[1] for v in ins.values()],
        out_specs=[v[1] for v in outs.values()],
        scratch_shapes=list(scratch.values()),
        compiler_params=pltpu.CompilerParams(
            vmem_limit_bytes=63 << 20,
            has_side_effects=remote,
            collective_id=0 if remote else None,
        ),
    )(*[v[0] for v in ins.values()])
    return dict(zip(outs, found))


def shards(
    images,
    tokens,
    slot_ids,
    counts,
    w_qkv,
    w_out,
    w_up,
    w_down,
    gain_one,
    bias_one,
    gain_two,
    bias_two,
    w_router,
    cotangent,
):
    features = tokens.shape[2]
    hidden = w_up.shape[1]
    parts = lax.axis_size("head")
    me = lax.axis_index("head")
    small = (gain_one, bias_one, gain_two, bias_two, w_router, cotangent)
    outer = images // 2 if images == 8 and parts == 4 else 0
    if outer:
        found = fused(
            parts, outer, tokens, slot_ids, counts, (w_qkv.T, w_out), w_up, w_down, *small
        )
        grads = found["grads_o"]
        part, rows = hidden // parts, w_out.shape[0]
        down, up, out, qkv, result, grad_tokens = finish(
            grads, (part, features, rows, grads.shape[0] - part - features - rows),
            found["result_o"], found["grad_tokens_o"],
        )
        qkv = qkv.T
        vectors = found["vec_o"]
    else:
        w_all = jnp.concatenate(
            [
                lax.all_gather(w_qkv.T, "head", axis=0, tiled=True),
                lax.all_gather(w_out, "head", axis=0, tiled=True),
            ]
        )
        found = fused(parts, outer, tokens, slot_ids, counts, (w_all,), w_up, w_down, *small)
        columns = w_all.shape[0] - features

        def reduced(matrix, axis=0):
            shard = lax.psum_scatter(matrix, "head", scatter_dimension=axis, tiled=True)
            piece = lax.psum_scatter(shard, "img", scatter_dimension=0, tiled=True)
            return lax.all_gather(piece, "img", axis=0, tiled=True).astype(F32)

        both = found["qkv_out_o"]
        down, up = reduced(found["down_o"]), reduced(found["up_o"], 1)
        out, qkv = reduced(both[columns:]), reduced(both[:columns]).T
        vectors = lax.psum(found["vec_o"], ("img", "head"))
        result, grad_tokens = found["result_o"], found["grad_tokens_o"]
    vectors = lax.dynamic_slice_in_dim(
        vectors, me * (features // parts), features // parts, axis=1
    )
    return (
        result,
        grad_tokens,
        qkv,
        out,
        up,
        down,
        vectors[0],
        vectors[1],
        vectors[2],
        vectors[3],
        vectors[4],
    )


def solution(mesh):
    return jax.shard_map(
        functools.partial(shards, mesh.shape["img"]),
        mesh=mesh,
        in_specs=(
            P(("img", "head"), None, None),
            P(("img", "head"), None),
            P(("img", "head")),
            P(None, "head"),
            P("head", None),
            P(),
            P(),
            P(),
            P(),
            P(),
            P(),
            P(),
            P(("img", "head"), None, None),
        ),
        out_specs=(
            P(("img", "head"), None, None),
            P(("img", "head"), None, None),
            P(None, "head"),
            P("head", None),
            P(None, "head"),
            P("head", None),
            P("head"),
            P("head"),
            P("head"),
            P("head"),
            P("head"),
        ),
        check_vma=False,
    )
```

profile of v0, /device:TPU:0, one launch (start us, length us, event | category | flops | bytes accessed | tf_op | source)
XLA Modules:
  0.0 183.6 jit_solution(12631469243895103808)
XLA Ops:
  0.7 173.0 %shard_map.212 = (bf16[6,197,768]{2,1,0:T(8,128)(2,1)}, f32[6,197,768]{2,1,0:T(8,128)}, f32[8,768]{1,0:T(8,128)}, bf16[960,3072]{1,0:T(8,128)(2,1)}, bf16[3072,7...) custom-call(s32[6,160]{1,0:T(8,128)} %refs_0_.1, s32[6]{0:T(128)} %refs_1_.1, f32[768]{0:T(1024)} %refs_2_.1, f32[768]{0:T(1024)} %refs_3_.1, ...), custom_call_target="tpu_custom_call" | custom-call | tf_op jit(solution)/shard_map/pallas_call | solution.py:983
  173.6 1.6 fusion
  175.2 8.3 %shard_map.213 = (f32[768,768]{1,0:T(8,128)}, f32[768,768]{1,0:T(8,128)}, f32[192,768]{1,0:T(8,128)}, f32[576,768]{1,0:T(8,128)}, bf16[6,197,768]{2,1,0:T(8,128)(2,1)}, /*index=5*/f32[6,197,768]{2,1,0:T(8,128)}) custom-call(bf16[2304,768]{1,0:T(8,128)(2,1)} %get-tuple-element.21.refs_0_, bf16[6,197,768]{2,1,0:T(8,128)(2,1)} %get-tuple-element.22.refs_1_, ...), custom_call_target="tpu_custom_call" | custom-call | tf_op jit(solution)/shard_map/pallas_call | solution.py:898
where the time goes:
time: 184 us
  Pallas kernels  181 us (98%)
    pallas_call x1, Pallas kernels, fused(): pl.pallas_call(functools.partial(fused_kernel, owned, length, capacity, p...  173 us
    pallas_call x1, Pallas kernels, finish(): pl.pallas_call(functools.partial(finish_kernel, sizes), out_shape=shapes,...  8.26 us

commit v1 on v0

--- a/solution.py
+++ b/solution.py
@@ -110,12 +110,9 @@
         self.core_at = (self.img, 2 * self.x + 1 - self.c)
         self.x_at = (self.img, self.across)
         self.y_at = (2 * self.z + 1 - self.y, self.head)
-        self.z_at = []
-        self.z_of = []
-        for k in range(1, outer):
-            other = lax.rem(self.z + k, outer)
-            self.z_of.append(other)
-            self.z_at.append((2 * other + self.y, self.head))
+        self.low, self.high = self.z % 2, self.z // 2
+        self.low_at = (2 * (self.z + 1 - 2 * self.low) + self.y, self.head)
+        self.high_at = (2 * (self.z + 2 - 4 * self.high) + self.y, self.head)
 
 
 def remote(source, target, sems, index, device):
@@ -150,7 +147,10 @@
         return self.whole.at[aligned(base, size or self.sizes[kind])]
 
     def first_row(self, side, t):
-        return side * AG_ROWS if t == self.split else (self.split * side + t) * AG_ROWS
+        if t == self.split:
+            return side * AG_ROWS
+        head = t + self.p.c * (self.split - 1 - 2 * t)
+        return (2 * head + side) * AG_ROWS
 
     def piece(self, shard, side, t):
         return self.part(shard, int(t == self.split), self.first_row(side, t), AG_ROWS)
@@ -234,14 +234,17 @@
         self.rows = [job[1] for job in jobs]
         self.target = [job[2] for job in jobs]
         self.base = [sum(self.rows[:j]) for j in range(len(jobs))]
-        self.from_core, self.from_x, self.from_y, self.from_z = buffers
-        self.core_sems, self.x_sems, self.y_sems, self.z_sems, self.az_sems, self.ay_sems = sems
+        self.from_core, self.from_x, self.from_y, self.from_low, self.from_high = buffers
+        self.core_sems, self.x_sems, self.y_sems, self.z_sems, self.a_sems = sems
         self.local_sem = local_sem
         self.jobs = len(jobs)
         self.sent = []
-        self.kept = []
-        self.core, self.over_x, self.over_y = {}, {}, {}
-        self.over_z, self.all_z, self.all_y = {}, {}, {}
+        self.kept, self.core, self.over_x, self.over_y = {}, {}, {}, {}
+        self.over_low, self.over_high = {}, {}
+        self.all_high, self.all_low, self.all_y = {}, {}, {}
+        self.steps = (
+            self.to_y, self.to_low, self.to_high, self.back_high, self.back_low, self.back_y, self.finish
+        )
         self.half = out.shape[1] // 2
         self.mine = aligned(place.y * self.half, self.half, 128)
         self.theirs = aligned((1 - place.y) * self.half, self.half, 128)
@@ -280,58 +283,70 @@
         )
         self.sent.append(self.over_y[j])
 
-    def quarters(self, j):
-        size = self.rows[j] // self.p.outer
-        base = self.base[j] // self.p.outer
-        return size, slice(base, base + size)
-
-    def to_z(self, j):
-        p = self.p
+    def piece(self, j, ref, base, lanes, level):
+        p, rows = self.p, self.rows[j]
+        if level == 0:
+            return ref.at[aligned(base, rows), lanes]
+        if level == 1:
+            return ref.at[aligned(base + p.low * (rows // 2), rows // 2), lanes]
+        return ref.at[aligned(base + p.low * (rows // 2) + p.high * (rows // 4), rows // 4), lanes]
+
+    def to_low(self, j):
+        p, half = self.p, self.rows[j] // 2
         self.over_y[j].wait_recv()
         block = self.blocks[j](p.own).at[:, self.mine]
         add_into(block, self.from_y.at[self.span(j)])
-        size, span = self.quarters(j)
-        self.over_z[j] = [
-            send(
-                block.at[aligned(size * p.z_of[k], size)], self.from_z.at[k, span],
-                self.z_sems, (j, k), p.z_at[k],
-            )
-            for k in range(p.outer - 1)
-        ]
-        self.sent += self.over_z[j]
-
-    def place_of(self, j, z, lanes):
-        size, _ = self.quarters(j)
-        return self.out.at[aligned(self.target[j] + size * z, size), lanes]
-
-    def spread(self, j):
-        p = self.p
-        for copy in self.over_z[j]:
-            copy.wait_recv()
-        size, span = self.quarters(j)
-        piece = self.blocks[j](p.own).at[aligned(size * p.z, size), self.mine]
-        add_into(piece, *[self.from_z.at[k, span] for k in range(p.outer - 1)])
-        target = self.place_of(j, p.z, self.mine)
-        self.kept.append(copy_in(piece, target, self.local_sem.at[j]))
-        self.all_z[j] = [
-            send(piece, target, self.az_sems, (j, k), p.z_at[k]) for k in range(p.outer - 1)
-        ]
-        self.all_y[j] = [send(piece, target, self.ay_sems, (j, 0), p.y_at)]
-        self.sent += self.all_z[j] + self.all_y[j]
-
-    def across_y(self, j):
-        p = self.p
-        for k in range(p.outer - 1):
-            self.all_z[j][k].wait_recv()
-            z = lax.rem(p.z + p.outer - 1 - k, p.outer)
-            block = self.place_of(j, z, self.mine)
-            copy = send(block, block, self.ay_sems, (j, k + 1), p.y_at)
-            self.all_y[j].append(copy)
-            self.sent.append(copy)
+        base = self.base[j] // 2
+        self.over_low[j] = send(
+            block.at[aligned((1 - p.low) * half, half)], self.from_low.at[base : base + half],
+            self.z_sems, (j, 0), p.low_at,
+        )
+        self.sent.append(self.over_low[j])
+
+    def to_high(self, j):
+        p, quarter = self.p, self.rows[j] // 4
+        self.over_low[j].wait_recv()
+        block = self.blocks[j](p.own)
+        base = self.base[j] // 2
+        add_into(
+            self.piece(j, block, 0, self.mine, 1), self.from_low.at[base : base + 2 * quarter]
+        )
+        base = self.base[j] // 4
+        self.over_high[j] = send(
+            block.at[aligned(p.low * 2 * quarter + (1 - p.high) * quarter, quarter), self.mine],
+            self.from_high.at[base : base + quarter], self.z_sems, (j, 1), p.high_at,
+        )
+        self.sent.append(self.over_high[j])
+
+    def spread(self, j, level, device, index):
+        block = self.piece(j, self.out, self.target[j], self.mine, level)
+        source = block
+        if level == 2:
+            source = self.piece(j, self.blocks[j](self.p.own), 0, self.mine, 2)
+        copy = send(source, block, self.a_sems, (j, index), device)
+        self.sent.append(copy)
+        return copy
+
+    def back_high(self, j):
+        self.over_high[j].wait_recv()
+        piece = self.piece(j, self.blocks[j](self.p.own), 0, self.mine, 2)
+        base, quarter = self.base[j] // 4, self.rows[j] // 4
+        add_into(piece, self.from_high.at[base : base + quarter])
+        target = self.piece(j, self.out, self.target[j], self.mine, 2)
+        self.kept[j] = copy_in(piece, target, self.local_sem.at[j])
+        self.all_high[j] = self.spread(j, 2, self.p.high_at, 0)
+
+    def back_low(self, j):
+        self.all_high[j].wait_recv()
+        self.kept[j].wait()
+        self.all_low[j] = self.spread(j, 1, self.p.low_at, 1)
+
+    def back_y(self, j):
+        self.all_low[j].wait_recv()
+        self.all_y[j] = self.spread(j, 0, self.p.y_at, 2)
 
     def finish(self, j):
-        for copy in self.all_y[j]:
-            copy.wait_recv()
+        self.all_y[j].wait_recv()
 
     def feed(self, last):
         for j in range(min(last + 1, self.jobs)):
@@ -339,25 +354,18 @@
                 self.to_x(j)
 
     def tick(self, t):
-        for lag, step in enumerate((self.to_y, self.to_z, self.spread, self.across_y, self.finish)):
+        for lag, step in enumerate(self.steps):
             if 0 <= t - lag < self.jobs:
                 step(t - lag)
 
     def close(self):
         for copy in self.sent:
             copy.wait_send()
-        for copy in self.kept:
-            copy.wait()
 
 
 def sum_vectors(place, vec, inbox, sems, sent):
     p = place
-    partners = [p.core_at, p.x_at, p.y_at]
-    bit = 1
-    while bit < p.outer:
-        low = lax.rem(p.z // bit, 2)
-        partners.append((2 * (p.z + bit - 2 * bit * low) + p.y, p.head))
-        bit *= 2
+    partners = [p.core_at, p.x_at, p.y_at, p.low_at, p.high_at]
     count = len(partners)
     copies = []
 
@@ -427,7 +435,7 @@
     if remote:
         place = Place(outer)
         barrier = pltpu.get_barrier_semaphore()
-        partners = [place.core_at, place.x_at, place.y_at, *place.z_at]
+        partners = [place.core_at, place.x_at, place.y_at, place.low_at, place.high_at]
         for partner in partners:
             pl.semaphore_signal(barrier, inc=1, device_id=partner, device_id_type=MESH_ID)
         pl.semaphore_wait(barrier, len(partners))
@@ -436,7 +444,6 @@
         )
         gather.begin()
         w_all = r["w_saved_o"]
-        half_order = (place.x, 1 - place.x)
 
         def rows_block(ref, base, step, rows):
             return lambda s: ref.at[aligned(s * step + base, rows)]
@@ -453,8 +460,7 @@
             (rows_block(down, piece * k, part, piece), piece, piece * k) for k in range(part // piece)
         ]
         jobs += [
-            (lanes_block(wu, features // 2 * k, features // 2), features // 2, part + features // 2 * k)
-            for k in range(2)
+            (lanes_block(wu, piece * k, piece), piece, part + piece * k) for k in range(features // piece)
         ]
         after = part + features
         jobs += [(rows_block(wd, columns, out_rows, out_rows), out_rows, after)]
@@ -464,16 +470,15 @@
             for q in range(3)
         ]
         reduce = Reduce(
-            place, jobs, r["grads_o"], [r[k] for k in ("from_core", "from_x", "from_y", "from_z")],
-            [(r[k + "_send"], r[k + "_recv"]) for k in ("core", "x", "y", "z", "az", "ay")],
+            place, jobs, r["grads_o"], [r[k] for k in ("from_core", "from_x", "from_y", "from_low", "from_high")],
+            [(r[k + "_send"], r[k + "_recv"]) for k in ("core", "x", "y", "z", "a")],
             r["kept_sems"],
         )
-        job_down, job_up = part // piece, 2
+        job_down, job_up = part // piece, features // piece
     else:
-        job_down, job_up = part // piece, 2
+        job_down, job_up = part // piece, 3
         w_all = r["w_all"]
         load_w = copy_in(w_all, down, sems.at[0])
-        half_order = (0, 1)
     load_up = copy_in(r["w_up"], wu, sems.at[1])
     load_down = copy_in(r["w_down"], wd, sems.at[2])
     ticks = [0]
@@ -505,20 +510,18 @@
         picked_grad[rows, :] = grads.astype(BF)
         grad_mlp[rows, :] = (gate * valid * grads).astype(BF)
 
-    def project(half):
-        base = pl.multiple_of(half * (columns // 2), 128)
-        size = rows_all // 3
+    def project(start, size):
+        step = rows_all // 3
 
         @pl.loop(0, 3)
         def _(n):
-            rows = aligned(n * size, size)
-            proj[rows, pl.ds(base, columns // 2)] = nt(
-                normed_one[rows, :], down[pl.ds(base, columns // 2), :]
-            ).astype(BF)
-
-    def attend(half, i):
+            rows = aligned(n * step, step)
+            cols = pl.ds(pl.multiple_of(start, 128), size)
+            proj[rows, cols] = nt(normed_one[rows, :], down[cols, :]).astype(BF)
+
+    def attend(half, chosen, i):
         rows = rows_of(i)
-        for p in range(pairs // 2):
+        for p in chosen:
             pair = half * (pairs // 2) + p
             tiles, swapped, low, zero, heads = pair_tiles(proj, rows, pair)
             outs = []
@@ -534,44 +537,62 @@
                 low, outs[0], outs[1]
             ).astype(BF)
 
+    half_columns = columns // 2
+    pair_columns = 6 * HEAD_DIM
     if remote:
         gather.forward_x(0)
         gather.own_half()
+        mine, other = place.x, 1 - place.x
     else:
         load_w.wait()
-
-    @pl.loop(0, 2)
-    def _(turn):
+        mine, other = 0, 1
+    project(mine * half_columns, half_columns)
+
+    @pl.loop(0, owned // 2)
+    def _(n):
+        i = 2 * n
         if remote:
-            half = place.x + turn - 2 * place.x * turn
-
-            @pl.when(turn == 1)
+            for at, steps in ((0, ((0, 1),)), (2, ((0, 2), (1, 0))), (4, ((1, 1),))):
+
+                @pl.when(i == at)
+                def _(steps=steps):
+                    for kind, t in steps:
+                        (gather.forward_y if kind else gather.forward_x)(t)
+
+        attend(mine, range(pairs // 2), i)
+        attend(mine, range(pairs // 2), i + 1)
+
+    if remote:
+        gather.other_half((0, 1))
+    for p in (0, 2):
+        project(other * half_columns + p * pair_columns, pair_columns)
+
+    if remote:
+        gather.forward_x(3)
+
+    @pl.loop(0, owned // 2)
+    def _(n):
+        if remote:
+
+            @pl.when(n == 1)
             def _():
                 gather.forward_y(2)
-                gather.other_half(range(gather.split))
-        else:
-            half = turn
-        project(half)
-
-        @pl.loop(0, owned)
-        def _(i):
-            if remote:
-                for at, steps in ((0, ((0, 1),)), (2, ((0, 2), (1, 0))), (4, ((1, 1),))):
-
-                    @pl.when((turn == 0) & (i == at))
-                    def _(steps=steps):
-                        for kind, t in steps:
-                            (gather.forward_y if kind else gather.forward_x)(t)
-
-                @pl.when((turn == 1) & (i == 0))
-                def _():
-                    gather.forward_x(3)
-
-                @pl.when((turn == 1) & (i == 3))
-                def _():
-                    gather.forward_y(3)
-
-            attend(half, i)
+
+            @pl.when(n == 2)
+            def _():
+                gather.forward_y(3)
+
+        attend(other, (0, 2), 2 * n)
+        attend(other, (0, 2), 2 * n + 1)
+
+    if remote:
+        gather.other_half((2,))
+    project(other * half_columns + pair_columns, pair_columns)
+
+    @pl.loop(0, owned // 3)
+    def _(n):
+        for k in range(3):
+            attend(other, (1,), 3 * n + k)
 
     if remote:
         gather.other_half((gather.split,))
@@ -690,9 +711,6 @@
         rows_f = picked[rows, :].astype(F32)
         gate, valid = row_gate(rows_f, w_router, counts[i])
         grads = picked_grad[rows, :].astype(F32)
-        logit = valid * gate * (1.0 - gate) * jnp.sum(grads * attn[rows, :], axis=-1, keepdims=True)
-        logits[rows, :] = jnp.broadcast_to(logit, (capacity, 128))
-        vec[0, 4:5, :] += jnp.sum(logit * rows_f, axis=0, keepdims=True)
         grad_mlp[rows, :] = (gate * valid * grads + wide[rows, :]).astype(BF)
 
     @pl.loop(0, 3)
@@ -748,23 +766,26 @@
 
     if remote:
         reduce.feed(job_down + job_up)
-    attend_back(early, 0, owned // 2)
-    tick()
-    attend_back(early, owned // 2, owned)
+    for n in range(3):
+        attend_back(early, n * owned // 3, (n + 1) * owned // 3)
+        if n < 2:
+            tick()
     grad_qkv(len(early), lambda n: n + (n + 1) // 2)
-    first_qkv = job_down + job_up + 1 if remote else 0
+    first_qkv = job_down + job_up + 1
     if remote:
         reduce.ready(first_qkv)
         reduce.ready(first_qkv + 1)
     tick()
-    attend_back(late, 0, owned // 2)
     if remote:
         reduce.feed(first_qkv + 1)
-    attend_back(late, owned // 2, owned)
+    attend_back(late, 0, owned)
     grad_qkv(len(late), lambda n: 3 * n + 1)
     if remote:
         reduce.ready(first_qkv + 2)
-    else:
+    tick()
+    if remote:
+        reduce.feed(first_qkv + 2)
+    if not remote:
         put_qkv = copy_in(wd, r["qkv_out_o"], sems.at[0])
 
     for n in range(3):
@@ -781,9 +802,16 @@
                 token_copy(i + 1, 1 - slot).start()
 
             rows = rows_of(i)
-            gate, valid = row_gate(picked[rows, :].astype(F32), w_router, counts[i])
+            rows_f = picked[rows, :].astype(F32)
+            gate, valid = row_gate(rows_f, w_router, counts[i])
+            branch = attn[rows, :]
+            logit = valid * gate * (1.0 - gate) * jnp.sum(
+                picked_grad[rows, :].astype(F32) * branch, axis=-1, keepdims=True
+            )
+            logits[rows, :] = jnp.broadcast_to(logit, (capacity, 128))
+            vec[0, 4:5, :] += jnp.sum(logit * rows_f, axis=0, keepdims=True)
             table = slot_table(slot_row(i), length)
-            upper, lower = split_low(gate * valid * attn[rows, :])
+            upper, lower = split_low(gate * valid * branch)
             token_copy(i, slot).wait()
 
             @pl.when(i >= 2)
@@ -794,8 +822,6 @@
             result_copy(i, slot).start()
 
     put_results(0, owned // 2)
-    if remote:
-        reduce.feed(first_qkv + 2)
     tick()
     put_results(owned // 2, owned)
 
@@ -810,39 +836,43 @@
             )
         attn[:, cols] = total
 
+    cot_copy(0, 0).start()
+
+    def put_gradients(first, last):
+        @pl.loop(first, last)
+        def _(i):
+            slot = lax.rem(i, 2)
+
+            @pl.when(i + 1 < owned)
+            def _():
+                cot_copy(i + 1, 1 - slot).start()
+
+            rows = rows_of(i)
+            rows_f = picked[rows, :].astype(F32)
+            unit, scale = standardise(rows_f)
+            grad = attn[rows, :]
+            vec[0, 0:1, :] += jnp.sum(grad * unit, axis=0, keepdims=True)
+            vec[0, 1:2, :] += jnp.sum(grad, axis=0, keepdims=True)
+            back = norm_pull(grad, unit, scale, gain_one)
+            total = back + wide[rows, :] + logits[rows, 0:1] * w_router
+            table = slot_table(slot_row(i), length)
+            upper, lower = split_low(total)
+            cot_copy(i, slot).wait()
+
+            @pl.when(i >= 2)
+            def _():
+                gtok_copy(i - 2, slot).wait()
+
+            gtok[slot] = cot[slot].astype(F32) + (nn(table, upper) + nn(table, lower))
+            gtok_copy(i, slot).start()
+
+    put_gradients(0, owned // 2)
     tick()
-    cot_copy(0, 0).start()
-
-    @pl.loop(0, owned)
-    def _(i):
-        slot = lax.rem(i, 2)
-
-        @pl.when(i + 1 < owned)
-        def _():
-            cot_copy(i + 1, 1 - slot).start()
-
-        rows = rows_of(i)
-        rows_f = picked[rows, :].astype(F32)
-        unit, scale = standardise(rows_f)
-        grad = attn[rows, :]
-        vec[0, 0:1, :] += jnp.sum(grad * unit, axis=0, keepdims=True)
-        vec[0, 1:2, :] += jnp.sum(grad, axis=0, keepdims=True)
-        back = norm_pull(grad, unit, scale, gain_one)
-        total = back + wide[rows, :] + logits[rows, 0:1] * w_router
-        table = slot_table(slot_row(i), length)
-        upper, lower = split_low(total)
-        cot_copy(i, slot).wait()
-
-        @pl.when(i >= 2)
-        def _():
-            gtok_copy(i - 2, slot).wait()
-
-        gtok[slot] = cot[slot].astype(F32) + (nn(table, upper) + nn(table, lower))
-        gtok_copy(i, slot).start()
+    put_gradients(owned // 2, owned)
 
     if remote:
         stages = sum_vectors(place, vec, r["vec_in"], (r["vec_send"], r["vec_recv"]), reduce.sent)
-        while ticks[0] < reduce.jobs + 4:
+        while ticks[0] < reduce.jobs + len(reduce.steps) - 1:
             if stages:
                 stages.pop(0)()
             tick()
@@ -941,7 +971,7 @@
     }
     steps = 3
     if remote:
-        steps = 3 + outer.bit_length() - 1
+        steps = 5
     scratch = {
         "wu": V((features, hidden), BF), "wd": V((hidden, features), BF), "ra": V((rows, hidden), BF),
         "rs": V((rows, hidden), BF), "down": V((hidden, features), BF),
@@ -959,18 +989,19 @@
         ins["w_out"] = (weights[1], outside)
         outs["w_saved_o"] = (S((columns + features, features), BF), outside)
         total = (columns + features + 2 * hidden) // parts
-        jobs = 9
+        jobs = 10
         outs["grads_o"] = (S((total, features), BF), outside)
         half = features // 2
         scratch.update({
             "from_core": V((2, total, features), BF), "from_x": V((total, features), BF),
-            "from_y": V((total, half), BF), "from_z": V((outer - 1, total // outer, half), BF),
+            "from_y": V((total, half), BF), "from_low": V((total // 2, half), BF),
+            "from_high": V((total // 4, half), BF),
             "vec_in": V((steps, 8, features), F32),
             "local_sems": D((2,)), "kept_sems": D((jobs,)),
         })
         for name, shape in (
-            ("ag", (18,)), ("core", (jobs, 2)), ("x", (jobs,)), ("y", (jobs,)), ("z", (jobs, outer - 1)),
-            ("az", (jobs, outer - 1)), ("ay", (jobs, outer)), ("vec", (steps,)),
+            ("ag", (18,)), ("core", (jobs, 2)), ("x", (jobs,)), ("y", (jobs,)), ("z", (jobs, 2)),
+            ("a", (jobs, 3)), ("vec", (steps,)),
         ):
             scratch[name + "_send"] = D(shape)
             scratch[name + "_recv"] = D(shape)

time: 184 us -> 181 us (0.984)
  Pallas kernels: 181 us -> 178 us
    pallas_call x1, Pallas kernels: 173 us -> 170 us  [fused(): pl.pallas_call(functools.partial(fused_kernel, owned, length, capacity, p...]
where the time goes in v1:
time: 181 us
  Pallas kernels  178 us (98%)
    pallas_call x1, Pallas kernels, fused(): pl.pallas_call(functools.partial(fused_kernel, owned, length, capacity, p...  170 us
    pallas_call x1, Pallas kernels, finish(): pl.pallas_call(functools.partial(finish_kernel, sizes), out_shape=shapes,...  8.26 us

profile of v1, /device:TPU:0, one launch (start us, length us, event | category | flops | bytes accessed | tf_op | source)
XLA Modules:
  0.0 180.7 jit_solution(13332164895729038060)
XLA Ops:
  0.7 170.0 %shard_map.212 = (bf16[6,197,768]{2,1,0:T(8,128)(2,1)}, f32[6,197,768]{2,1,0:T(8,128)}, f32[8,768]{1,0:T(8,128)}, bf16[960,3072]{1,0:T(8,128)(2,1)}, bf16[3072,7...) custom-call(s32[6,160]{1,0:T(8,128)} %refs_0_.1, s32[6]{0:T(128)} %refs_1_.1, f32[768]{0:T(1024)} %refs_2_.1, f32[768]{0:T(1024)} %refs_3_.1, ...), custom_call_target="tpu_custom_call" | custom-call | tf_op jit(solution)/shard_map/pallas_call | solution.py:1014
  170.7 1.6 fusion
  172.2 8.3 %shard_map.213 = (f32[768,768]{1,0:T(8,128)}, f32[768,768]{1,0:T(8,128)}, f32[192,768]{1,0:T(8,128)}, f32[576,768]{1,0:T(8,128)}, bf16[6,197,768]{2,1,0:T(8,128)(2,1)}, /*index=5*/f32[6,197,768]{2,1,0:T(8,128)}) custom-call(bf16[2304,768]{1,0:T(8,128)(2,1)} %get-tuple-element.21.refs_0_, bf16[6,197,768]{2,1,0:T(8,128)(2,1)} %get-tuple-element.22.refs_1_, ...), custom_call_target="tpu_custom_call" | custom-call | tf_op jit(solution)/shard_map/pallas_call | solution.py:928

commit v2 on v1

--- a/solution.py
+++ b/solution.py
@@ -730,10 +730,12 @@
     reload.wait()
 
     def attend_back(chosen, first, last):
-        @pl.loop(first, last)
-        def _(i):
-            rows = rows_of(i)
-            for pair in chosen:
+        each = 4 // len(chosen) if len(chosen) < 4 else 1
+
+        @pl.loop(first // each, last // each)
+        def _(n):
+            for i, pair in [(each * n + k, pair) for k in range(each) for pair in chosen]:
+                rows = rows_of(i)
                 tiles, swapped, low, zero, heads = pair_tiles(proj, rows, pair)
                 lanes = slice(2 * HEAD_DIM * pair, 2 * HEAD_DIM * (pair + 1))
                 grads = normed_two[rows, lanes]

time: 181 us -> 181 us (level)
  no operation moved by 1% of the time
where the time goes in v2:
time: 181 us
  Pallas kernels  179 us (99%)
    pallas_call x1, Pallas kernels, fused(): pl.pallas_call(functools.partial(fused_kernel, owned, length, capacity, p...  170 us
    pallas_call x1, Pallas kernels, finish(): pl.pallas_call(functools.partial(finish_kernel, sizes), out_shape=shapes,...  8.26 us

profile of v2, /device:TPU:0, one launch (start us, length us, event | category | flops | bytes accessed | tf_op | source)
XLA Modules:
  0.0 180.9 jit_solution(8316277475577329591)
XLA Ops:
  0.7 170.3 %shard_map.212 = (bf16[6,197,768]{2,1,0:T(8,128)(2,1)}, f32[6,197,768]{2,1,0:T(8,128)}, f32[8,768]{1,0:T(8,128)}, bf16[960,3072]{1,0:T(8,128)(2,1)}, bf16[3072,7...) custom-call(s32[6,160]{1,0:T(8,128)} %refs_0_.1, s32[6]{0:T(128)} %refs_1_.1, f32[768]{0:T(1024)} %refs_2_.1, f32[768]{0:T(1024)} %refs_3_.1, ...), custom_call_target="tpu_custom_call" | custom-call | tf_op jit(solution)/shard_map/pallas_call | solution.py:1016
  170.9 1.6 fusion
  172.5 8.3 %shard_map.213 = (f32[768,768]{1,0:T(8,128)}, f32[768,768]{1,0:T(8,128)}, f32[192,768]{1,0:T(8,128)}, f32[576,768]{1,0:T(8,128)}, bf16[6,197,768]{2,1,0:T(8,128)(2,1)}, /*index=5*/f32[6,197,768]{2,1,0:T(8,128)}) custom-call(bf16[2304,768]{1,0:T(8,128)(2,1)} %get-tuple-element.21.refs_0_, bf16[6,197,768]{2,1,0:T(8,128)(2,1)} %get-tuple-element.22.refs_1_, ...), custom_call_target="tpu_custom_call" | custom-call | tf_op jit(solution)/shard_map/pallas_call | solution.py:930
